TPU v7x, 128 devices: a whole 4x4x4 slice. The times are simulated.
128 devices in a mesh: grp: 4 (over x), dev: 32 (over z, y, core).
Axes of the slice: x: 4, y: 4, z: 4, core: 2. Of those that a mesh axis runs over, the one named last changes fastest.
Arguments:
- tracers: float32 [72, 8, 32, 4096], P(None, None, 'grp', 'dev'), may hold values from -6 to 6
- wind_east: float32 [72, 32, 4096], P(None, 'grp', 'dev'), may hold values from -1 to 1
- wind_north: float32 [72, 32, 4096], P(None, 'grp', 'dev'), may hold values from -1 to 1
- point_mass: float32 [32, 4096], P('grp', 'dev'), may hold values from 0.5 to 2
- diffusivity: float32 [72, 128, 2048], P(None, ('grp', 'dev')), may hold values from 0.05 to 2000
- destination: int32 [128, 1024, 1], P(('grp', 'dev')), may hold values from 0 to 127; in each aligned block of 1024 rows (0 to 1023, 1024 to 2047, ..., all dimensions but the last counted through in order) at most 16 rows name the same one
- column_cost: int32 [128, 1024], P(('grp', 'dev')), may hold values from 1 to 3
Outputs:
- mixed_tracers: float32 [72, 8, 32, 4096], P(None, None, 'grp', 'dev')
- bottom_values: float32 [8, 128, 2048], P(None, ('grp', 'dev'))
Inputs may be any that keep to these rules, and one draw needn't show every extreme that they name: `destination`: each owner sends at most 16 of its columns to one physics device, and in every draw some owner sends exactly 16 to one device.
All inputs are finite; a program needn't handle non-finite values.
Results may differ from a plain program's by a relative error of at most 0.0003.
Values sent between devices are 32-bit elements; how exact they have to be, the bound alone decides.
A program may use at most 128 MiB of HBM per device.

v0:
```python
import jax
import jax.numpy as jnp
import numpy as np
from jax import lax
from jax.experimental import pallas as pl
from jax.experimental.pallas import tpu as pltpu
from jax.sharding import PartitionSpec as P

LEV = 72
TRC = 8
ROWS = LEV * TRC * 8
GRP = 4
DEV = 32
ALL = GRP * DEV
CUTS = ((0, 25), (25, 49), (49, 73))
MESH = pl.DeviceIdType.MESH
F32 = jnp.float32
BF16 = jnp.bfloat16


def gll_derivative():
    points = np.array([-1.0, -1.0 / np.sqrt(5.0), 1.0 / np.sqrt(5.0), 1.0])
    der = np.zeros((4, 4))
    for i in range(4):
        for k in range(4):
            others = [m for m in range(4) if m != k]
            if i == k:
                der[i, k] = sum(1.0 / (points[k] - points[m]) for m in others)
            else:
                term = 1.0
                for m in others:
                    if m != i:
                        term *= (points[i] - points[m]) / (points[k] - points[m])
                der[i, k] = term / (points[k] - points[i])
    return der


def north_weights():
    along = np.kron(np.eye(32), gll_derivative().T).astype(np.float32)
    high = along.astype(jnp.bfloat16)
    low = (along - high.astype(np.float32)).astype(jnp.bfloat16)
    return np.block([[high, low], [high, np.zeros_like(low)]])


def iota(shape, dim):
    return lax.broadcasted_iota(jnp.int32, shape, dim)


def swap_blocks(values):
    row, lane = iota((8, 128), 0), iota((8, 128), 1)
    turned = pltpu.roll(values, 0, 1, stride=16, stride_axis=0)
    moved = jnp.take_along_axis(turned, (lane // 16 - row + 8) % 8, axis=0, mode="promise_in_bounds")
    return jnp.take_along_axis(moved, (lane + 16 * row) % 128, axis=1, mode="promise_in_bounds")


def halves(values):
    high = values.astype(BF16)
    return high, (values - high.astype(F32)).astype(BF16)


def kernel(
    tr_h, we_h, wn_h, pm_h, df_h, dst_h, cst_h, w_h, out, bot,
    tr, we, wn, pm, df, dst, cst, w, xb, rb, vb, hx, acc, hy, hd, uh, minv, av, onehot, lhs, kc,
    inv_t, low_t, up_t, inv_b, low_b, up_b, sb, rbm,
    local_sem, ks, kr, ko, hs, hr, ys, yr, ds, dr, bs, br, bo,
):
    g, d = lax.axis_index("grp"), lax.axis_index("dev")
    me = g * DEV + d
    der = gll_derivative().astype(np.float32)

    def peer(k):
        p = lax.rem(me + k, ALL)
        return p, (lax.div(p, DEV), lax.rem(p, DEV))

    loads = [
        pltpu.make_async_copy(src, dst_ref, local_sem.at[i])
        for i, (src, dst_ref) in enumerate(
            ((df_h, df), (tr_h, tr), (we_h, we), (wn_h, wn), (pm_h, pm), (w_h, w), (dst_h, dst), (cst_h, cst))
        )
    ]
    for copy in loads:
        copy.start()

    barrier = pltpu.get_barrier_semaphore()

    def greet(k, carry):
        pl.semaphore_signal(barrier, inc=1, device_id=peer(k)[1], device_id_type=MESH)
        return carry

    lax.fori_loop(1, ALL, greet, 0)

    loads[0].wait()
    xb2, rb2 = xb.reshape(ALL * 16, 128), rb.reshape(ALL * 16, 128)

    def pack(tile, carry):
        for group in range(9):
            rows = df[pl.ds(group * 128 + tile, 8, stride=16), :]
            xb2[pl.ds(tile * 128 + group, 8, stride=16), :] = swap_blocks(rows)
        return carry

    lax.fori_loop(0, 16, pack, 0)
    own = pltpu.make_async_copy(xb.at[me, pl.ds(0, 9)], rb.at[me, pl.ds(0, 9)], ko)
    own.start()
    pl.semaphore_wait(barrier, ALL - 1)

    def send_kappa(k, carry):
        p, where = peer(k)
        pltpu.make_async_remote_copy(
            xb.at[p, pl.ds(0, 9)], rb.at[me, pl.ds(0, 9)], ks, kr, device_id=where, device_id_type=MESH
        ).start()
        return carry

    lax.fori_loop(1, ALL, send_kappa, 0)

    for copy in loads[1:]:
        copy.wait()
    for x in range(8):
        vb[0, x] = jnp.broadcast_to(pm[x : x + 1, :], (8, 128))

    def advect(block, carry):
        first = block * 8
        cells = [
            [tr[pl.ds((first + j) * 64 + x, 8, stride=8), :] for x in range(8)] for j in range(8)
        ]
        stacked = jnp.concatenate([c for level in cells for c in level], axis=0)
        product = jnp.dot(jnp.concatenate(halves(stacked), axis=1), w[...], preferred_element_type=F32)
        north = product[:, :128] + product[:, 128:]
        for j in range(8):
            for x in range(8):
                base = x // 4 * 4
                east = sum(float(der[x % 4, k]) * cells[j][base + k] for k in range(4))
                at = pl.ds((first + j) * 8 + x, 1)
                row = (j * 8 + x) * 8
                moved = cells[j][x] - (we[at, :] * east + wn[at, :] * north[row : row + 8])
                vb[1 + first + j, x] = pm[x : x + 1, :] * moved
        return carry

    row_copies = []
    for part, (lo, hi) in enumerate(CUTS):
        lax.fori_loop(3 * part, 3 * part + 3, advect, 0)
        span = pl.ds(lo, hi - lo)
        pair = []
        for side, (x, step) in enumerate(((7, 1), (0, GRP - 1))):
            copy = pltpu.make_async_remote_copy(
                vb.at[span, x], hx.at[side, span], hs.at[side, part], hr.at[side, part],
                device_id=(lax.rem(g + step, GRP), d), device_id_type=MESH,
            )
            copy.start()
            pair.append(copy)
        row_copies.append(pair)

    lane = iota((8, 128), 1)

    def gather_edges(x, carry):
        first = last = jnp.zeros((8, 128), F32)
        for s in range(LEV + 1):
            value = vb[s, x]
            first = jnp.where(lane == s, pltpu.roll(value, s, 1), first)
            last = jnp.where(lane == s, pltpu.roll(value, s + 1, 1), last)
        acc[0, x] = first
        acc[1, x] = last
        return carry

    lax.fori_loop(0, 8, gather_edges, 0)
    up_g, down_g = lax.rem(g + 1, GRP), lax.rem(g + GRP - 1, GRP)
    up_d, down_d = lax.rem(d + 1, DEV), lax.rem(d + DEV - 1, DEV)
    edge_copies = [
        pltpu.make_async_remote_copy(src, to, s, r, device_id=where, device_id_type=MESH)
        for src, to, s, r, where in (
            (acc.at[1], hy.at[0], ys.at[0], yr.at[0], (g, up_d)),
            (acc.at[0], hy.at[1], ys.at[1], yr.at[1], (g, down_d)),
            (acc.at[1, 7], hd.at[0], ds.at[0], dr.at[0], (up_g, up_d)),
            (acc.at[1, 0], hd.at[1], ds.at[1], dr.at[1], (down_g, up_d)),
            (acc.at[0, 7], hd.at[2], ds.at[2], dr.at[2], (up_g, down_d)),
            (acc.at[0, 0], hd.at[3], ds.at[3], dr.at[3], (down_g, down_d)),
        )
    ]
    for copy in edge_copies:
        copy.start()

    devices = iota((ALL, 128), 0)
    earlier = jnp.concatenate(
        [(iota((128, 128), 0) < iota((128, 128), 1)).astype(F32), jnp.ones((128, 128), F32)], axis=1
    ).astype(BF16)

    def place(x, before):
        target = jnp.broadcast_to(dst[pl.ds(x, 1), :], (ALL, 128))
        match = (target == devices).astype(F32)
        counts = jnp.dot(match.astype(BF16), earlier, preferred_element_type=F32)
        rank = jnp.sum((counts[:, :128] + before) * match, axis=0, keepdims=True)
        slot = dst[pl.ds(x, 1), :] * 16 + rank.astype(jnp.int32)
        at = pl.ds(pl.multiple_of(x * 128, 128), 128)

        def fill(block, carry):
            rows = block * 256 + iota((256, 128), 0)
            hit = (rows == jnp.broadcast_to(slot, (256, 128))).astype(F32)
            onehot[pl.ds(pl.multiple_of(block * 256, 256), 256), at] = hit.astype(BF16)
            return carry

        lax.fori_loop(0, 8, fill, 0)
        return before + counts[:, 128:]

    lax.fori_loop(0, 8, place, jnp.zeros((ALL, 128), F32))

    for copy in edge_copies:
        copy.wait()
    for side in range(2):
        uh[side, 0] = hy[side, 0] + hd[2 * side]
        uh[side, 7] = hy[side, 7] + hd[2 * side + 1]
        middle = hy[side, 3] + hy[side, 4]
        for x in (1, 2, 5, 6):
            uh[side, x] = hy[side, x]
        uh[side, 3] = middle
        uh[side, 4] = middle

    own.wait()
    sized = rb.at[pl.ds(0, ALL - 1), pl.ds(0, 9)]
    pltpu.make_async_copy(sized, sized, kr).wait()

    def unpack(tile, carry):
        at = pl.ds(pl.multiple_of(tile * 128, 128), 128)
        for group in range(9):
            values = swap_blocks(rb2[pl.ds(tile * 128 + group, 8, stride=16), :])
            rest = values - values.astype(BF16).astype(F32)
            lhs[group * 16 : group * 16 + 16, at] = jnp.concatenate([values, rest], axis=0).astype(BF16)
        return carry

    lax.fori_loop(0, 16, unpack, 0)

    def columns(x, carry):
        at = pl.ds(pl.multiple_of(x * 256, 256), 256)
        found = jnp.dot(lhs[...], onehot[:, at], preferred_element_type=F32)
        for group in range(9):
            whole = found[group * 16 : group * 16 + 8] + found[group * 16 + 8 : group * 16 + 16]
            for half in range(2):
                kc[pl.ds(group * 64 + 2 * x + half, 8, stride=8), :] = whole[:, half * 128 : half * 128 + 128]
        return carry

    lax.fori_loop(0, 4, columns, 0)

    def tile(k):
        return pl.ds(pl.multiple_of(k * 8, 8), 8)

    def eliminate(i, carry):
        gain_t, h_t, gain_b, h_b = carry
        k = i
        kk = LEV - 1 - i
        next_t = jnp.where(k < LEV - 1, 0.5 * (kc[tile(k), :] + kc[tile(jnp.minimum(k + 1, LEV - 1)), :]), 0.0)
        e = 1.0 + gain_t
        inv = 1.0 / (e + next_t)
        inv_t[tile(k), :] = inv
        low_t[tile(k), :] = h_t * inv
        up = next_t * inv
        up_t[tile(k), :] = up
        next_b = jnp.where(kk > 0, 0.5 * (kc[tile(kk), :] + kc[tile(jnp.maximum(kk - 1, 0)), :]), 0.0)
        e_b = 1.0 + gain_b
        inv2 = 1.0 / (e_b + next_b)
        inv_b[tile(kk), :] = inv2
        low_b[tile(kk), :] = h_b * inv2
        up2 = next_b * inv2
        up_b[tile(kk), :] = up2
        return up * e, next_t, up2 * e_b, next_b

    zero = jnp.zeros((8, 128), F32)
    lax.fori_loop(0, LEV, eliminate, (zero,) * 4)

    start_lane, end_lane = lane == 0, lane == 127
    at_first, at_last = lane % 4 == 0, lane % 4 == 3

    def edge_sum(s):
        u = [vb[s, x] for x in range(8)]
        u[0] = u[0] + hx[0, s]
        u[7] = u[7] + hx[1, s]
        u[3] = u[3] + u[4]
        result = [None] * 8
        for x in (0, 1, 2, 3, 5, 6, 7):
            from_left = pltpu.roll(uh[0, x], lax.rem(128 - s, 128), 1)
            from_right = pltpu.roll(uh[1, x], 127 - s, 1)
            left = jnp.where(start_lane, from_left, pltpu.roll(u[x], 1, 1))
            right = jnp.where(end_lane, from_right, pltpu.roll(u[x], 127, 1))
            result[x] = u[x] + jnp.where(at_first, left, jnp.where(at_last, right, 0.0))
        result[4] = result[3]
        return result

    for part, (lo, hi) in enumerate(CUTS):
        for copy in row_copies[part]:
            copy.wait_recv()
        if part == 0:
            for x, value in enumerate(edge_sum(jnp.int32(0))):
                minv[x] = 1.0 / value

        def average(s, carry):
            for x, value in enumerate(edge_sum(s)):
                av[pl.ds((s - 1) * 64 + x, 8, stride=8), :] = value * minv[x]
            return carry

        lax.fori_loop(max(lo, 1), hi, average, 0)

    def at_level(k, f):
        return pl.ds(pl.multiple_of(k * 64 + f * 8, 8), 8)

    def sweep_1(k, previous):
        inv, low = inv_t[tile(k), :], low_t[tile(k), :]
        current = tuple(av[at_level(k, f), :] * inv + low * previous[f] for f in range(TRC))
        for f in range(TRC):
            av[at_level(k, f), :] = current[f]
        return current

    lax.fori_loop(0, LEV, sweep_1, (zero,) * TRC)
    second, third = cst[...] >= 2, cst[...] >= 3

    def sweep_2(i, carry):
        following, previous = carry
        k = LEV - 1 - i
        up = up_t[tile(k), :]
        inv = jnp.where(second, inv_b[tile(k), :], 1.0)
        low = jnp.where(second, low_b[tile(k), :], 0.0)
        solved = tuple(av[at_level(k, f), :] + up * following[f] for f in range(TRC))
        current = tuple(solved[f] * inv + low * previous[f] for f in range(TRC))
        for f in range(TRC):
            av[at_level(k, f), :] = current[f]
        return solved, current

    lax.fori_loop(0, LEV, sweep_2, ((zero,) * TRC, (zero,) * TRC))

    def sweep_3(k, carry):
        following, previous = carry
        up = jnp.where(second, up_b[tile(k), :], 0.0)
        inv = jnp.where(third, inv_t[tile(k), :], 1.0)
        low = jnp.where(third, low_t[tile(k), :], 0.0)
        solved = tuple(av[at_level(k, f), :] + up * following[f] for f in range(TRC))
        current = tuple(solved[f] * inv + low * previous[f] for f in range(TRC))
        for f in range(TRC):
            av[at_level(k, f), :] = current[f]
        return solved, current

    lax.fori_loop(0, LEV, sweep_3, ((zero,) * TRC, (zero,) * TRC))

    last = jnp.concatenate(
        [av[pl.ds((LEV - 1) * 64 + x, 8, stride=8), :] for x in range(8)], axis=1
    )
    rest = last - last.astype(BF16).astype(F32)
    both = jnp.concatenate([last, rest], axis=0).astype(BF16)
    for block in range(8):
        spread = lax.dot_general(
            both, onehot[block * 256 : block * 256 + 256, :], (((1,), (1,)), ((), ())), preferred_element_type=F32
        )
        whole = spread[:8] + spread[8:]
        for half in range(2):
            at = (2 * block + half) * 8
            sb[at : at + 8, :] = swap_blocks(whole[:, half * 128 : half * 128 + 128])
    own_bottom = pltpu.make_async_copy(sb.at[me], rbm.at[me], bo)
    own_bottom.start()

    def send_bottom(k, carry):
        p, where = peer(k)
        pltpu.make_async_remote_copy(
            sb.at[p], rbm.at[me], bs, br, device_id=where, device_id_type=MESH
        ).start()
        return carry

    lax.fori_loop(1, ALL, send_bottom, 0)

    def sweep_4(i, following):
        k = LEV - 1 - i
        up = jnp.where(third, up_t[tile(k), :], 0.0)
        solved = tuple(av[at_level(k, f), :] + up * following[f] for f in range(TRC))
        for f in range(TRC):
            out[at_level(k, f), :] = solved[f]
        return solved

    lax.fori_loop(0, LEV, sweep_4, (zero,) * TRC)

    own_bottom.wait()
    sized = rbm.at[pl.ds(0, ALL - 1)]
    pltpu.make_async_copy(sized, sized, br).wait()
    for t in range(16):
        bot[pl.ds(t, 8, stride=16), :] = swap_blocks(rbm[t * 8 : t * 8 + 8, :])

    for pair in row_copies:
        for copy in pair:
            copy.wait_send()
    sized = xb.at[pl.ds(0, ALL - 1), pl.ds(0, 9)]
    pltpu.make_async_copy(sized, sized, ks).wait()
    sized = sb.at[pl.ds(0, ALL - 1)]
    pltpu.make_async_copy(sized, sized, bs).wait()


def shards(tracers, wind_east, wind_north, point_mass, diffusivity, destination, column_cost):
    weights = jnp.asarray(north_weights())
    vmem = pltpu.VMEM
    dma = pltpu.SemaphoreType.DMA
    mixed, bottoms = pl.pallas_call(
        kernel,
        out_shape=[jax.ShapeDtypeStruct((ROWS, 128), F32), jax.ShapeDtypeStruct((128, 128), F32)],
        in_specs=[pl.BlockSpec(memory_space=pl.ANY)] * 8,
        out_specs=[pl.BlockSpec(memory_space=vmem)] * 2,
        scratch_shapes=[
            vmem((ROWS, 128), F32),
            vmem((LEV * 8, 128), F32),
            vmem((LEV * 8, 128), F32),
            vmem((8, 128), F32),
            vmem((LEV * 16, 128), F32),
            vmem((8, 128), jnp.int32),
            vmem((8, 128), jnp.int32),
            vmem((256, 256), BF16),
            vmem((ALL, 16, 128), F32),
            vmem((ALL, 16, 128), F32),
            vmem((LEV + 1, 8, 8, 128), F32),
            vmem((2, LEV + 1, 8, 128), F32),
            vmem((2, 8, 8, 128), F32),
            vmem((2, 8, 8, 128), F32),
            vmem((4, 8, 128), F32),
            vmem((2, 8, 8, 128), F32),
            vmem((8, 8, 128), F32),
            vmem((ROWS, 128), F32),
            vmem((ALL * 16, 1024), BF16),
            vmem((LEV * 2, ALL * 16), BF16),
            vmem((LEV * 8, 128), F32),
        ]
        + [vmem((LEV * 8, 128), F32)] * 6
        + [vmem((128, 128), F32)] * 2
        + [dma((8,)), dma, dma, dma, dma((2, 3)), dma((2, 3)), dma((2,)), dma((2,)), dma((4,)), dma((4,)), dma, dma, dma],
        compiler_params=pltpu.CompilerParams(
            collective_id=0, has_side_effects=True, vmem_limit_bytes=48 * 2**20
        ),
        cost_estimate=pl.CostEstimate(flops=2 * 10**9, bytes_accessed=7 * 10**6, transcendentals=0),
        name="tracer_step",
    )(
        tracers.reshape(ROWS, 128),
        wind_east.reshape(LEV * 8, 128),
        wind_north.reshape(LEV * 8, 128),
        point_mass,
        diffusivity.reshape(LEV * 16, 128),
        destination.reshape(8, 128),
        column_cost.reshape(8, 128),
        weights,
    )
    return mixed.reshape(LEV, TRC, 8, 128), bottoms.reshape(TRC, 1, ALL * 16)


def solution(mesh):
    return jax.shard_map(
        shards,
        mesh=mesh,
        in_specs=(
            P(None, None, "grp", "dev"),
            P(None, "grp", "dev"),
            P(None, "grp", "dev"),
            P("grp", "dev"),
            P(None, ("grp", "dev"), None),
            P(("grp", "dev"), None, None),
            P(("grp", "dev"), None),
        ),
        out_specs=(P(None, None, "grp", "dev"), P(None, ("grp", "dev"), None)),
        check_vma=False,
    )
```

profile of v0, /device:TPU:1, one launch (start us, length us, event | category | flops | bytes accessed | tf_op | source)
XLA Modules:
  0.0 60.3 jit_solution(6685360262890650182)
XLA Ops:
  0.6 0.0 copy-start
  0.6 1.7 %copy-done = f32[72,8,8,128]{3,2,1,0:T(8,128)S(1)} copy-done((f32[72,8,8,128]{3,2,1,0:T(8,128)S(1)}, f32[72,8,8,128]{3,2,1,0:T(8,128)}, u32[]{:S(2)}) %copy-start) | copy-done | bytes 2359320
  2.3 0.0 copy-start.1
  2.3 1.1 %copy-done.1 = f32[72,1,2048]{2,1,0:T(1,128)S(1)} copy-done((f32[72,1,2048]{2,1,0:T(1,128)S(1)}, f32[72,1,2048]{2,1,0:T(1,128)}, u32[]{:S(2)}) %copy-start.1) | copy-done | bytes 589848
  3.4 0.0 copy-start.2
  3.4 1.0 %copy-done.2 = f32[72,8,128]{2,1,0:T(8,128)S(1)} copy-done((f32[72,8,128]{2,1,0:T(8,128)S(1)}, f32[72,8,128]{2,1,0:T(8,128)}, u32[]{:S(2)}) %copy-start.2) | copy-done | bytes 294936
  4.3 0.0 copy-start.3
  4.3 1.0 %copy-done.3 = f32[72,8,128]{2,1,0:T(8,128)S(1)} copy-done((f32[72,8,128]{2,1,0:T(8,128)S(1)}, f32[72,8,128]{2,1,0:T(8,128)}, u32[]{:S(2)}) %copy-start.3) | copy-done | bytes 294936
  5.3 0.0 copy-start.4
  5.3 0.7 %copy-done.4 = f32[8,128]{1,0:T(8,128)S(1)} copy-done((f32[8,128]{1,0:T(8,128)S(1)}, f32[8,128]{1,0:T(8,128)}, u32[]{:S(2)}) %copy-start.4) | copy-done | bytes 4120
  6.0 0.0 copy-start.5
  6.0 0.7 %copy-done.5 = s32[1,1024,1]{1,2,0:T(1,128)S(1)} copy-done((s32[1,1024,1]{1,2,0:T(1,128)S(1)}, s32[1,1024,1]{1,2,0:T(1,128)}, u32[]{:S(2)}) %copy-start.5) | copy-done | bytes 4120
  6.7 0.0 copy-start.6
  6.7 0.7 %copy-done.6 = s32[1,1024]{1,0:T(1,128)S(1)} copy-done((s32[1,1024]{1,0:T(1,128)S(1)}, s32[1,1024]{1,0:T(1,128)}, u32[]{:S(2)}) %copy-start.6) | copy-done | bytes 4120
  7.3 0.0 copy-start.7
  7.4 0.9 %copy-done.7 = bf16[256,256]{1,0:T(8,128)(2,1)S(1)} copy-done((bf16[256,256]{1,0:T(8,128)(2,1)S(1)}, bf16[256,256]{1,0:T(8,128)(2,1)}, u32[]{:S(2)}) %copy-start.7) | copy-done | bytes 131096
  8.3 50.0 %tracer_step.1 = (f32[4608,128]{1,0:T(8,128)S(1)}, f32[128,128]{1,0:T(8,128)S(1)}) custom-call(f32[4608,128]{1,0:T(8,128)S(1)} %bitcast.10, f32[576,128]{1,0:T(8,128)S(1)} %bitcast.12, f32[576,128]{1,0:T(8,128)S(1)} %bitcast.13, f32[8,128]{1,0:T(8,128)S(1)} %copy-done.4, f32[1152,128]{1,0:T(8,128)S(1)} %bitcast.11, s32[8,128]{1,0:T(8,128)S(1)} %bitcast.14, ...), custom_call_target="tpu_custom_call" | custom-call | flops 2000000000 | bytes 7000000 | tf_op jit(solution)/shard_map/tracer_step/pallas_call | solution.py:393
  58.3 1.4 %copy.13 = f32[72,8,8,128]{3,2,1,0:T(8,128)} copy(f32[72,8,8,128]{3,2,1,0:T(8,128)S(1)} %bitcast.8) | data formatting | bytes 4718592
  59.7 0.6 %copy.14 = f32[8,1,2048]{2,1,0:T(1,128)} copy(f32[8,1,2048]{2,1,0:T(1,128)S(1)} %bitcast.9) | data formatting | bytes 131072
Async XLA Ops:
  0.6 1.7 %copy-start = (f32[72,8,8,128]{3,2,1,0:T(8,128)S(1)}, f32[72,8,8,128]{3,2,1,0:T(8,128)}, u32[]{:S(2)}) copy-start(f32[72,8,8,128]{3,2,1,0:T(8,128)} %param.8) | copy-start | bytes 7077892
  2.3 1.1 %copy-start.1 = (f32[72,1,2048]{2,1,0:T(1,128)S(1)}, f32[72,1,2048]{2,1,0:T(1,128)}, u32[]{:S(2)}) copy-start(f32[72,1,2048]{2,1,0:T(1,128)} %param.12) | copy-start | bytes 1769476
  3.4 1.0 %copy-start.2 = (f32[72,8,128]{2,1,0:T(8,128)S(1)}, f32[72,8,128]{2,1,0:T(8,128)}, u32[]{:S(2)}) copy-start(f32[72,8,128]{2,1,0:T(8,128)} %param.9) | copy-start | bytes 884740
  4.3 1.0 %copy-start.3 = (f32[72,8,128]{2,1,0:T(8,128)S(1)}, f32[72,8,128]{2,1,0:T(8,128)}, u32[]{:S(2)}) copy-start(f32[72,8,128]{2,1,0:T(8,128)} %param.10) | copy-start | bytes 884740
  5.3 0.7 %copy-start.4 = (f32[8,128]{1,0:T(8,128)S(1)}, f32[8,128]{1,0:T(8,128)}, u32[]{:S(2)}) copy-start(f32[8,128]{1,0:T(8,128)} %pm_h.1) | copy-start | bytes 12292
  6.0 0.7 %copy-start.5 = (s32[1,1024,1]{1,2,0:T(1,128)S(1)}, s32[1,1024,1]{1,2,0:T(1,128)}, u32[]{:S(2)}) copy-start(s32[1,1024,1]{1,2,0:T(1,128)} %param.13) | copy-start | bytes 12292
  6.7 0.7 %copy-start.6 = (s32[1,1024]{1,0:T(1,128)S(1)}, s32[1,1024]{1,0:T(1,128)}, u32[]{:S(2)}) copy-start(s32[1,1024]{1,0:T(1,128)} %param.14) | copy-start | bytes 12292
  7.3 0.9 %copy-start.7 = (bf16[256,256]{1,0:T(8,128)(2,1)S(1)}, bf16[256,256]{1,0:T(8,128)(2,1)}, u32[]{:S(2)}) copy-start(bf16[256,256]{1,0:T(8,128)(2,1)} %constant.2.clone.w_h) | copy-start | bytes 393220
where the time goes:
time: 60.7 us; the launch traced here: 60.3 us
  Pallas kernels  50 us (82%)
  local copies, waits for them, and re-layouts  9.64 us (16%)
  between operations  0.66 us (1%)
    pallas_call x1, Pallas kernels, shards(): pl.pallas_call(kernel, out_shape=[jax.ShapeDtypeStruct((ROWS, 128), F32),...  50 us
    unnamed x18, local copies, waits for them, and re-layouts  9.64 us

commit v1 on v0

--- a/solution.py
+++ b/solution.py
@@ -98,7 +98,7 @@
             xb2[pl.ds(tile * 128 + group, 8, stride=16), :] = swap_blocks(rows)
         return carry
 
-    lax.fori_loop(0, 16, pack, 0)
+    lax.fori_loop(0, 16, pack, 0, unroll=2)
     own = pltpu.make_async_copy(xb.at[me, pl.ds(0, 9)], rb.at[me, pl.ds(0, 9)], ko)
     own.start()
     pl.semaphore_wait(barrier, ALL - 1)
@@ -213,6 +213,33 @@
         uh[side, 3] = middle
         uh[side, 4] = middle
 
+    start_lane, end_lane = lane == 0, lane == 127
+    at_first, at_last = lane % 4 == 0, lane % 4 == 3
+
+    def across(s, x, u):
+        from_left = pltpu.roll(uh[0, x], lax.rem(128 - s, 128), 1)
+        from_right = pltpu.roll(uh[1, x], 127 - s, 1)
+        left = jnp.where(start_lane, from_left, pltpu.roll(u, 1, 1))
+        right = jnp.where(end_lane, from_right, pltpu.roll(u, 127, 1))
+        return u + jnp.where(at_first, left, jnp.where(at_last, right, 0.0))
+
+    def inner_sum(s):
+        middle = across(s, 3, vb[s, 3] + vb[s, 4])
+        return [(3, middle), (4, middle)] + [(x, across(s, x, vb[s, x])) for x in (1, 2, 5, 6)]
+
+    def outer_sum(s):
+        return [(x, across(s, x, vb[s, x] + hx[side, s])) for side, x in ((0, 0), (1, 7))]
+
+    for x, value in inner_sum(jnp.int32(0)):
+        minv[x] = 1.0 / value
+
+    def average_inner(s, carry):
+        for x, value in inner_sum(s):
+            av[pl.ds((s - 1) * 64 + x, 8, stride=8), :] = value * minv[x]
+        return carry
+
+    lax.fori_loop(1, LEV + 1, average_inner, 0, unroll=4)
+
     own.wait()
     sized = rb.at[pl.ds(0, ALL - 1), pl.ds(0, 9)]
     pltpu.make_async_copy(sized, sized, kr).wait()
@@ -225,7 +252,7 @@
             lhs[group * 16 : group * 16 + 16, at] = jnp.concatenate([values, rest], axis=0).astype(BF16)
         return carry
 
-    lax.fori_loop(0, 16, unpack, 0)
+    lax.fori_loop(0, 16, unpack, 0, unroll=2)
 
     def columns(x, carry):
         at = pl.ds(pl.multiple_of(x * 256, 256), 256)
@@ -262,39 +289,21 @@
         return up * e, next_t, up2 * e_b, next_b
 
     zero = jnp.zeros((8, 128), F32)
-    lax.fori_loop(0, LEV, eliminate, (zero,) * 4)
-
-    start_lane, end_lane = lane == 0, lane == 127
-    at_first, at_last = lane % 4 == 0, lane % 4 == 3
-
-    def edge_sum(s):
-        u = [vb[s, x] for x in range(8)]
-        u[0] = u[0] + hx[0, s]
-        u[7] = u[7] + hx[1, s]
-        u[3] = u[3] + u[4]
-        result = [None] * 8
-        for x in (0, 1, 2, 3, 5, 6, 7):
-            from_left = pltpu.roll(uh[0, x], lax.rem(128 - s, 128), 1)
-            from_right = pltpu.roll(uh[1, x], 127 - s, 1)
-            left = jnp.where(start_lane, from_left, pltpu.roll(u[x], 1, 1))
-            right = jnp.where(end_lane, from_right, pltpu.roll(u[x], 127, 1))
-            result[x] = u[x] + jnp.where(at_first, left, jnp.where(at_last, right, 0.0))
-        result[4] = result[3]
-        return result
+    lax.fori_loop(0, LEV, eliminate, (zero,) * 4, unroll=4)
 
     for part, (lo, hi) in enumerate(CUTS):
         for copy in row_copies[part]:
             copy.wait_recv()
         if part == 0:
-            for x, value in enumerate(edge_sum(jnp.int32(0))):
+            for x, value in outer_sum(jnp.int32(0)):
                 minv[x] = 1.0 / value
 
-        def average(s, carry):
-            for x, value in enumerate(edge_sum(s)):
+        def average_outer(s, carry):
+            for x, value in outer_sum(s):
                 av[pl.ds((s - 1) * 64 + x, 8, stride=8), :] = value * minv[x]
             return carry
 
-        lax.fori_loop(max(lo, 1), hi, average, 0)
+        lax.fori_loop(max(lo, 1), hi, average_outer, 0, unroll=4)
 
     def at_level(k, f):
         return pl.ds(pl.multiple_of(k * 64 + f * 8, 8), 8)
@@ -306,7 +315,7 @@
             av[at_level(k, f), :] = current[f]
         return current
 
-    lax.fori_loop(0, LEV, sweep_1, (zero,) * TRC)
+    lax.fori_loop(0, LEV, sweep_1, (zero,) * TRC, unroll=4)
     second, third = cst[...] >= 2, cst[...] >= 3
 
     def sweep_2(i, carry):
@@ -321,7 +330,7 @@
             av[at_level(k, f), :] = current[f]
         return solved, current
 
-    lax.fori_loop(0, LEV, sweep_2, ((zero,) * TRC, (zero,) * TRC))
+    lax.fori_loop(0, LEV, sweep_2, ((zero,) * TRC, (zero,) * TRC), unroll=4)
 
     def sweep_3(k, carry):
         following, previous = carry
@@ -334,7 +343,7 @@
             av[at_level(k, f), :] = current[f]
         return solved, current
 
-    lax.fori_loop(0, LEV, sweep_3, ((zero,) * TRC, (zero,) * TRC))
+    lax.fori_loop(0, LEV, sweep_3, ((zero,) * TRC, (zero,) * TRC), unroll=4)
 
     last = jnp.concatenate(
         [av[pl.ds((LEV - 1) * 64 + x, 8, stride=8), :] for x in range(8)], axis=1
@@ -369,7 +378,7 @@
             out[at_level(k, f), :] = solved[f]
         return solved
 
-    lax.fori_loop(0, LEV, sweep_4, (zero,) * TRC)
+    lax.fori_loop(0, LEV, sweep_4, (zero,) * TRC, unroll=4)
 
     own_bottom.wait()
     sized = rbm.at[pl.ds(0, ALL - 1)]
@@ -393,7 +402,7 @@
     mixed, bottoms = pl.pallas_call(
         kernel,
         out_shape=[jax.ShapeDtypeStruct((ROWS, 128), F32), jax.ShapeDtypeStruct((128, 128), F32)],
-        in_specs=[pl.BlockSpec(memory_space=pl.ANY)] * 8,
+        in_specs=[pl.BlockSpec(memory_space=pltpu.HBM)] * 8,
         out_specs=[pl.BlockSpec(memory_space=vmem)] * 2,
         scratch_shapes=[
             vmem((ROWS, 128), F32),
@@ -422,7 +431,7 @@
         + [vmem((128, 128), F32)] * 2
         + [dma((8,)), dma, dma, dma, dma((2, 3)), dma((2, 3)), dma((2,)), dma((2,)), dma((4,)), dma((4,)), dma, dma, dma],
         compiler_params=pltpu.CompilerParams(
-            collective_id=0, has_side_effects=True, vmem_limit_bytes=48 * 2**20
+            collective_id=0, has_side_effects=True, vmem_limit_bytes=63 * 2**20
         ),
         cost_estimate=pl.CostEstimate(flops=2 * 10**9, bytes_accessed=7 * 10**6, transcendentals=0),
         name="tracer_step",

time: 60.7 us -> 51.2 us (0.84)
  local copies, waits for them, and re-layouts: 9.64 us -> 4.02 us
  Pallas kernels: 50 us -> 46.4 us
    unnamed x18 -> x4, local copies, waits for them, and re-layouts: 9.64 us -> 4.02 us
    pallas_call x1, Pallas kernels: 50 us -> 46.4 us  [shards(): pl.pallas_call(kernel, out_shape=[jax.ShapeDtypeStruct((ROWS, 128), F32),...]
where the time goes in v1:
time: 51.2 us; the launch traced here: 51.1 us
  Pallas kernels  46.4 us (91%)
  local copies, waits for them, and re-layouts  4.02 us (8%)
  between operations  0.65 us (1%)
    pallas_call x1, Pallas kernels, shards(): pl.pallas_call(kernel, out_shape=[jax.ShapeDtypeStruct((ROWS, 128), F32),...  46.4 us
    unnamed x4, local copies, waits for them, and re-layouts  4.02 us

profile of v1, /device:TPU:1, one launch (start us, length us, event | category | flops | bytes accessed | tf_op | source)
XLA Modules:
  0.0 51.1 jit_solution(6880339896896662958)
XLA Ops:
  0.6 46.4 %tracer_step.1 = (f32[4608,128]{1,0:T(8,128)}, f32[128,128]{1,0:T(8,128)}) custom-call(f32[4608,128]{1,0:T(8,128)} %bitcast.10, f32[576,128]{1,0:T(8,128)} %bitcast.12, f32[576,128]{1,0:T(8,128)} %bitcast.13, f32[8,128]{1,0:T(8,128)} %pm_h.1, f32[1152,128]{1,0:T(8,128)} %bitcast.11, s32[8,128]{1,0:T(8,128)} %bitcast.14, s32[8,128]{1,0:T(8,128)} %bitcast.15, ...), custom_call_target="tpu_custom_call" | custom-call | flops 2000000000 | bytes 7000000 | tf_op jit(solution)/shard_map/tracer_step/pallas_call | solution.py:402
  47.0 0.0 copy-start
  47.1 3.4 %copy.13 = f32[72,8,8,128]{3,2,1,0:T(8,128)} copy(f32[72,8,8,128]{3,2,1,0:T(8,128)} %bitcast.8) | data formatting | bytes 4718592
  50.4 0.0 copy-done
  50.4 0.6 %copy.14 = f32[8,1,2048]{2,1,0:T(1,128)} copy(f32[8,1,2048]{2,1,0:T(1,128)S(1)} %bitcast.9) | data formatting | bytes 131072
Async XLA Ops:
  47.0 3.4 %copy-start = (f32[128,128]{1,0:T(8,128)S(1)}, f32[128,128]{1,0:T(8,128)}, u32[]{:S(2)}) copy-start(f32[128,128]{1,0:T(8,128)} %get-tuple-element.5) | copy-start | bytes 196612

commit v2 on v1

--- a/solution.py
+++ b/solution.py
@@ -46,11 +46,12 @@
     return lax.broadcasted_iota(jnp.int32, shape, dim)
 
 
-def swap_blocks(values):
+def swap_blocks(values, last=False):
     row, lane = iota((8, 128), 0), iota((8, 128), 1)
     turned = pltpu.roll(values, 0, 1, stride=16, stride_axis=0)
     moved = jnp.take_along_axis(turned, (lane // 16 - row + 8) % 8, axis=0, mode="promise_in_bounds")
-    return jnp.take_along_axis(moved, (lane + 16 * row) % 128, axis=1, mode="promise_in_bounds")
+    source = lane % 8 * 16 + lane // 8 if last else lane
+    return jnp.take_along_axis(moved, (source + 16 * row) % 128, axis=1, mode="promise_in_bounds")
 
 
 def halves(values):
@@ -59,18 +60,36 @@
 
 
 def kernel(
-    tr_h, we_h, wn_h, pm_h, df_h, dst_h, cst_h, w_h, out, bot,
-    tr, we, wn, pm, df, dst, cst, w, xb, rb, vb, hx, acc, hy, hd, uh, minv, av, onehot, lhs, kc,
-    inv_t, low_t, up_t, inv_b, low_b, up_b, sb, rbm,
+    tr_h, we_h, wn_h, pm_h, df_h, dst_h, cst_h, w_h, out, rbm,
+    tr, we, wn, pm, df, dst, cst, w, xb, rb, vb, hx, acc, hy, hd, uh, minv, av, rank, chosen_by, lhs, spread, kc,
+    inv_t, low_t, up_t, inv_b, low_b, up_b, sb,
     local_sem, ks, kr, ko, hs, hr, ys, yr, ds, dr, bs, br, bo,
 ):
     g, d = lax.axis_index("grp"), lax.axis_index("dev")
     me = g * DEV + d
     der = gll_derivative().astype(np.float32)
 
-    def peer(k):
-        p = lax.rem(me + k, ALL)
-        return p, (lax.div(p, DEV), lax.rem(p, DEV))
+    z, y, core = lax.div(d, 8), lax.rem(lax.div(d, 2), 4), lax.rem(d, 2)
+
+    def eight(step, t, act, count=8):
+        to_g, to_z = lax.rem(g + step, GRP), lax.rem(z + t + 1, 4)
+        for i in range(count):
+            to_d = to_z * 8 + lax.rem(y + i // 2 + 1, 4) * 2 + lax.rem(core + i + 1, 2)
+            act(to_g * DEV + to_d, (to_g, to_d))
+
+    def for_peers(act, beside=None):
+        for turn, step in enumerate((2, 1, 3, 0)):
+
+            def some(t, carry):
+                eight(step, t, act)
+                if beside is not None:
+                    beside(4 * turn + t)
+                return carry
+
+            lax.fori_loop(0, 3 if step == 0 else 4, some, 0)
+        eight(0, 3, act, 7)
+        if beside is not None:
+            beside(15)
 
     loads = [
         pltpu.make_async_copy(src, dst_ref, local_sem.at[i])
@@ -83,34 +102,20 @@
 
     barrier = pltpu.get_barrier_semaphore()
 
-    def greet(k, carry):
-        pl.semaphore_signal(barrier, inc=1, device_id=peer(k)[1], device_id_type=MESH)
-        return carry
-
-    lax.fori_loop(1, ALL, greet, 0)
+    def greet(p, where):
+        pl.semaphore_signal(barrier, inc=1, device_id=where, device_id_type=MESH)
 
     loads[0].wait()
     xb2, rb2 = xb.reshape(ALL * 16, 128), rb.reshape(ALL * 16, 128)
 
-    def pack(tile, carry):
+    def pack(tile):
         for group in range(9):
             rows = df[pl.ds(group * 128 + tile, 8, stride=16), :]
-            xb2[pl.ds(tile * 128 + group, 8, stride=16), :] = swap_blocks(rows)
-        return carry
-
-    lax.fori_loop(0, 16, pack, 0, unroll=2)
+            xb2[pl.ds(tile * 128 + group, 8, stride=16), :] = swap_blocks(rows, last=True)
+
+    for_peers(greet, pack)
     own = pltpu.make_async_copy(xb.at[me, pl.ds(0, 9)], rb.at[me, pl.ds(0, 9)], ko)
     own.start()
-    pl.semaphore_wait(barrier, ALL - 1)
-
-    def send_kappa(k, carry):
-        p, where = peer(k)
-        pltpu.make_async_remote_copy(
-            xb.at[p, pl.ds(0, 9)], rb.at[me, pl.ds(0, 9)], ks, kr, device_id=where, device_id_type=MESH
-        ).start()
-        return carry
-
-    lax.fori_loop(1, ALL, send_kappa, 0)
 
     for copy in loads[1:]:
         copy.wait()
@@ -135,28 +140,16 @@
                 vb[1 + first + j, x] = pm[x : x + 1, :] * moved
         return carry
 
-    row_copies = []
-    for part, (lo, hi) in enumerate(CUTS):
-        lax.fori_loop(3 * part, 3 * part + 3, advect, 0)
-        span = pl.ds(lo, hi - lo)
-        pair = []
-        for side, (x, step) in enumerate(((7, 1), (0, GRP - 1))):
-            copy = pltpu.make_async_remote_copy(
-                vb.at[span, x], hx.at[side, span], hs.at[side, part], hr.at[side, part],
-                device_id=(lax.rem(g + step, GRP), d), device_id_type=MESH,
-            )
-            copy.start()
-            pair.append(copy)
-        row_copies.append(pair)
+    lax.fori_loop(0, 9, advect, 0)
 
     lane = iota((8, 128), 1)
 
     def gather_edges(x, carry):
         first = last = jnp.zeros((8, 128), F32)
         for s in range(LEV + 1):
-            value = vb[s, x]
-            first = jnp.where(lane == s, pltpu.roll(value, s, 1), first)
-            last = jnp.where(lane == s, pltpu.roll(value, s + 1, 1), last)
+            value = pltpu.roll(vb[s, x], s + 1, 1)
+            first = jnp.where(lane == s + 1, value, first)
+            last = jnp.where(lane == s, value, last)
         acc[0, x] = first
         acc[1, x] = last
         return carry
@@ -175,53 +168,69 @@
             (acc.at[0, 0], hd.at[3], ds.at[3], dr.at[3], (down_g, down_d)),
         )
     ]
+    pl.semaphore_wait(barrier, ALL - 1)
     for copy in edge_copies:
         copy.start()
+
+    def send_kappa(p, where):
+        pltpu.make_async_remote_copy(
+            xb.at[p, pl.ds(0, 9)], rb.at[me, pl.ds(0, 9)], ks, kr, device_id=where, device_id_type=MESH
+        ).start()
+
+    for_peers(send_kappa)
+    row_copies = [
+        [
+            pltpu.make_async_remote_copy(
+                vb.at[pl.ds(lo, hi - lo), x], hx.at[side, pl.ds(lo, hi - lo)], hs.at[side, part], hr.at[side, part],
+                device_id=(to_g, d), device_id_type=MESH,
+            )
+            for side, (x, to_g) in enumerate(((7, up_g), (0, down_g)))
+        ]
+        for part, (lo, hi) in enumerate(CUTS)
+    ]
+    for pair in row_copies:
+        for copy in pair:
+            copy.start()
 
     devices = iota((ALL, 128), 0)
     earlier = jnp.concatenate(
         [(iota((128, 128), 0) < iota((128, 128), 1)).astype(F32), jnp.ones((128, 128), F32)], axis=1
     ).astype(BF16)
-
-    def place(x, before):
-        target = jnp.broadcast_to(dst[pl.ds(x, 1), :], (ALL, 128))
-        match = (target == devices).astype(F32)
-        counts = jnp.dot(match.astype(BF16), earlier, preferred_element_type=F32)
-        rank = jnp.sum((counts[:, :128] + before) * match, axis=0, keepdims=True)
-        slot = dst[pl.ds(x, 1), :] * 16 + rank.astype(jnp.int32)
-        at = pl.ds(pl.multiple_of(x * 128, 128), 128)
-
-        def fill(block, carry):
-            rows = block * 256 + iota((256, 128), 0)
-            hit = (rows == jnp.broadcast_to(slot, (256, 128))).astype(F32)
-            onehot[pl.ds(pl.multiple_of(block * 256, 256), 256), at] = hit.astype(BF16)
-            return carry
-
-        lax.fori_loop(0, 8, fill, 0)
-        return before + counts[:, 128:]
-
-    lax.fori_loop(0, 8, place, jnp.zeros((ALL, 128), F32))
+    before = jnp.zeros((ALL, 128), F32)
+    for x in range(8):
+        match = (jnp.broadcast_to(dst[x : x + 1, :], (ALL, 128)) == devices).astype(F32)
+        chosen = match.astype(BF16)
+        counts = jnp.dot(chosen, earlier, preferred_element_type=F32)
+        order = jnp.sum((counts[:, :128] + before) * match, axis=0, keepdims=True)
+        rank[x : x + 1, :] = order.astype(jnp.int32)
+        at = slice(x * 128, x * 128 + 128)
+        chosen_by[:ALL, at] = chosen
+        chosen_by[ALL:, at] = chosen
+        before = before + counts[:, 128:]
 
     for copy in edge_copies:
         copy.wait()
+    sides = []
     for side in range(2):
-        uh[side, 0] = hy[side, 0] + hd[2 * side]
-        uh[side, 7] = hy[side, 7] + hd[2 * side + 1]
         middle = hy[side, 3] + hy[side, 4]
-        for x in (1, 2, 5, 6):
-            uh[side, x] = hy[side, x]
-        uh[side, 3] = middle
-        uh[side, 4] = middle
-
-    start_lane, end_lane = lane == 0, lane == 127
+        rows = [hy[side, x] for x in range(8)]
+        rows[0] = rows[0] + hd[2 * side]
+        rows[7] = rows[7] + hd[2 * side + 1]
+        rows[3] = rows[4] = middle
+        sides.append(rows)
+    even = lane % 2 == 0
+    for x in range(8):
+        from_left, from_right = sides[0][x], pltpu.roll(sides[1][x], 126, 1)
+        uh[0, x] = jnp.where(even, from_left, from_right)
+        uh[1, x] = jnp.where(even, from_right, from_left)
+
     at_first, at_last = lane % 4 == 0, lane % 4 == 3
+    at_end, at_side = (lane == 0) | (lane == 127), at_first | at_last
 
     def across(s, x, u):
-        from_left = pltpu.roll(uh[0, x], lax.rem(128 - s, 128), 1)
-        from_right = pltpu.roll(uh[1, x], 127 - s, 1)
-        left = jnp.where(start_lane, from_left, pltpu.roll(u, 1, 1))
-        right = jnp.where(end_lane, from_right, pltpu.roll(u, 127, 1))
-        return u + jnp.where(at_first, left, jnp.where(at_last, right, 0.0))
+        halo = pltpu.roll(uh[lax.rem(s, 2), x], lax.rem(128 - s, 128), 1)
+        beside = jnp.where(at_first, pltpu.roll(u, 1, 1), pltpu.roll(u, 127, 1))
+        return u + jnp.where(at_side, jnp.where(at_end, halo, beside), 0.0)
 
     def inner_sum(s):
         middle = across(s, 3, vb[s, 3] + vb[s, 4])
@@ -244,23 +253,23 @@
     sized = rb.at[pl.ds(0, ALL - 1), pl.ds(0, 9)]
     pltpu.make_async_copy(sized, sized, kr).wait()
 
-    def unpack(tile, carry):
-        at = pl.ds(pl.multiple_of(tile * 128, 128), 128)
-        for group in range(9):
-            values = swap_blocks(rb2[pl.ds(tile * 128 + group, 8, stride=16), :])
-            rest = values - values.astype(BF16).astype(F32)
-            lhs[group * 16 : group * 16 + 16, at] = jnp.concatenate([values, rest], axis=0).astype(BF16)
-        return carry
-
-    lax.fori_loop(0, 16, unpack, 0, unroll=2)
-
-    def columns(x, carry):
-        at = pl.ds(pl.multiple_of(x * 256, 256), 256)
-        found = jnp.dot(lhs[...], onehot[:, at], preferred_element_type=F32)
-        for group in range(9):
-            whole = found[group * 16 : group * 16 + 8] + found[group * 16 + 8 : group * 16 + 16]
-            for half in range(2):
-                kc[pl.ds(group * 64 + 2 * x + half, 8, stride=8), :] = whole[:, half * 128 : half * 128 + 128]
+    for group in range(9):
+        values = rb2[pl.ds(group, ALL, stride=16), :].T
+        lhs[group * 128 : group * 128 + 128, :] = jnp.concatenate(halves(values), axis=1)
+
+    def columns(pair, carry):
+        at = pl.ds(pl.multiple_of(pair * 256, 256), 256)
+        found = jnp.dot(lhs[...], chosen_by[:, at], preferred_element_type=F32)
+        for half in range(2):
+            x = 2 * pair + half
+            order = jnp.broadcast_to(rank[pl.ds(x, 1), :], (8, 128))
+            hits = [order == r for r in range(16)]
+            for group in range(9):
+                value = found[group * 128 : group * 128 + 8, half * 128 : half * 128 + 128]
+                for r in range(1, 16):
+                    row = group * 128 + r * 8
+                    value = jnp.where(hits[r], found[row : row + 8, half * 128 : half * 128 + 128], value)
+                kc[pl.ds(group * 64 + x, 8, stride=8), :] = value
         return carry
 
     lax.fori_loop(0, 4, columns, 0)
@@ -289,8 +298,7 @@
         return up * e, next_t, up2 * e_b, next_b
 
     zero = jnp.zeros((8, 128), F32)
-    lax.fori_loop(0, LEV, eliminate, (zero,) * 4, unroll=4)
-
+    carry = (zero,) * 4
     for part, (lo, hi) in enumerate(CUTS):
         for copy in row_copies[part]:
             copy.wait_recv()
@@ -298,12 +306,12 @@
             for x, value in outer_sum(jnp.int32(0)):
                 minv[x] = 1.0 / value
 
-        def average_outer(s, carry):
+        def both(s, carry):
             for x, value in outer_sum(s):
                 av[pl.ds((s - 1) * 64 + x, 8, stride=8), :] = value * minv[x]
-            return carry
-
-        lax.fori_loop(max(lo, 1), hi, average_outer, 0, unroll=4)
+            return eliminate(s - 1, carry)
+
+        carry = lax.fori_loop(max(lo, 1), hi, both, carry, unroll=4)
 
     def at_level(k, f):
         return pl.ds(pl.multiple_of(k * 64 + f * 8, 8), 8)
@@ -345,30 +353,29 @@
 
     lax.fori_loop(0, LEV, sweep_3, ((zero,) * TRC, (zero,) * TRC), unroll=4)
 
-    last = jnp.concatenate(
-        [av[pl.ds((LEV - 1) * 64 + x, 8, stride=8), :] for x in range(8)], axis=1
+    slots = iota((16, 128), 0)
+    for f in range(TRC):
+        base = av[(LEV - 1) * 64 + f * 8 : (LEV - 1) * 64 + f * 8 + 8, :]
+        rest = base - base.astype(BF16).astype(F32)
+        for x in range(8):
+            hit = jnp.broadcast_to(rank[x : x + 1, :], (16, 128)) == slots
+            for part, value in enumerate((base, rest)):
+                spread[part * 128 + f * 16 : part * 128 + f * 16 + 16, x * 128 : x * 128 + 128] = jnp.where(
+                    hit, jnp.broadcast_to(value[x : x + 1, :], (16, 128)), 0.0
+                ).astype(BF16)
+    placed = lax.dot_general(
+        chosen_by[:ALL, :], spread[...], (((1,), (1,)), ((), ())), preferred_element_type=F32
     )
-    rest = last - last.astype(BF16).astype(F32)
-    both = jnp.concatenate([last, rest], axis=0).astype(BF16)
-    for block in range(8):
-        spread = lax.dot_general(
-            both, onehot[block * 256 : block * 256 + 256, :], (((1,), (1,)), ((), ())), preferred_element_type=F32
-        )
-        whole = spread[:8] + spread[8:]
-        for half in range(2):
-            at = (2 * block + half) * 8
-            sb[at : at + 8, :] = swap_blocks(whole[:, half * 128 : half * 128 + 128])
+    sb[...] = placed[:, :128] + placed[:, 128:]
     own_bottom = pltpu.make_async_copy(sb.at[me], rbm.at[me], bo)
     own_bottom.start()
 
-    def send_bottom(k, carry):
-        p, where = peer(k)
+    def send_bottom(p, where):
         pltpu.make_async_remote_copy(
             sb.at[p], rbm.at[me], bs, br, device_id=where, device_id_type=MESH
         ).start()
-        return carry
-
-    lax.fori_loop(1, ALL, send_bottom, 0)
+
+    for_peers(send_bottom)
 
     def sweep_4(i, following):
         k = LEV - 1 - i
@@ -383,9 +390,6 @@
     own_bottom.wait()
     sized = rbm.at[pl.ds(0, ALL - 1)]
     pltpu.make_async_copy(sized, sized, br).wait()
-    for t in range(16):
-        bot[pl.ds(t, 8, stride=16), :] = swap_blocks(rbm[t * 8 : t * 8 + 8, :])
-
     for pair in row_copies:
         for copy in pair:
             copy.wait_send()
@@ -395,13 +399,39 @@
     pltpu.make_async_copy(sized, sized, bs).wait()
 
 
+def finish(mixed, received, out, bot, held, sem):
+    part = ROWS // 8
+    copies = [
+        pltpu.make_async_copy(mixed.at[pl.ds(i * part, part)], out.at[pl.ds(i * part, part)], sem.at[i])
+        for i in range(8)
+    ]
+    for copy in copies:
+        copy.start()
+    for t in range(16):
+        held[pl.ds(t, 8, stride=16), :] = swap_blocks(received[t * 8 : t * 8 + 8, :])
+    copies.append(pltpu.make_async_copy(held, bot, sem.at[8]))
+    copies[-1].start()
+    for copy in copies:
+        copy.wait()
+
+
 def shards(tracers, wind_east, wind_north, point_mass, diffusivity, destination, column_cost):
     weights = jnp.asarray(north_weights())
     vmem = pltpu.VMEM
     dma = pltpu.SemaphoreType.DMA
-    mixed, bottoms = pl.pallas_call(
+    operands = (
+        tracers.reshape(ROWS, 128),
+        wind_east.reshape(LEV * 8, 128),
+        wind_north.reshape(LEV * 8, 128),
+        point_mass,
+        diffusivity.reshape(LEV * 16, 128),
+        destination.reshape(8, 128),
+        column_cost.reshape(8, 128),
+        weights,
+    )
+    mixed, received = pl.pallas_call(
         kernel,
-        out_shape=[jax.ShapeDtypeStruct((ROWS, 128), F32), jax.ShapeDtypeStruct((128, 128), F32)],
+        out_shape=[vmem((ROWS, 128), F32), vmem((128, 128), F32)],
         in_specs=[pl.BlockSpec(memory_space=pltpu.HBM)] * 8,
         out_specs=[pl.BlockSpec(memory_space=vmem)] * 2,
         scratch_shapes=[
@@ -423,28 +453,31 @@
             vmem((2, 8, 8, 128), F32),
             vmem((8, 8, 128), F32),
             vmem((ROWS, 128), F32),
-            vmem((ALL * 16, 1024), BF16),
-            vmem((LEV * 2, ALL * 16), BF16),
+            vmem((8, 128), jnp.int32),
+            vmem((2 * ALL, 1024), BF16),
+            vmem((LEV * 16, 2 * ALL), BF16),
+            vmem((256, 1024), BF16),
             vmem((LEV * 8, 128), F32),
         ]
         + [vmem((LEV * 8, 128), F32)] * 6
-        + [vmem((128, 128), F32)] * 2
+        + [vmem((128, 128), F32)]
         + [dma((8,)), dma, dma, dma, dma((2, 3)), dma((2, 3)), dma((2,)), dma((2,)), dma((4,)), dma((4,)), dma, dma, dma],
         compiler_params=pltpu.CompilerParams(
-            collective_id=0, has_side_effects=True, vmem_limit_bytes=63 * 2**20
+            collective_id=0, has_side_effects=True, vmem_limit_bytes=48 * 2**20
         ),
         cost_estimate=pl.CostEstimate(flops=2 * 10**9, bytes_accessed=7 * 10**6, transcendentals=0),
         name="tracer_step",
-    )(
-        tracers.reshape(ROWS, 128),
-        wind_east.reshape(LEV * 8, 128),
-        wind_north.reshape(LEV * 8, 128),
-        point_mass,
-        diffusivity.reshape(LEV * 16, 128),
-        destination.reshape(8, 128),
-        column_cost.reshape(8, 128),
-        weights,
-    )
+    )(*(pltpu.with_memory_space_constraint(value, pltpu.HBM) for value in operands))
+    mixed, bottoms = pl.pallas_call(
+        finish,
+        out_shape=[jax.ShapeDtypeStruct((ROWS, 128), F32), jax.ShapeDtypeStruct((128, 128), F32)],
+        in_specs=[pl.BlockSpec(memory_space=vmem)] * 2,
+        out_specs=[pl.BlockSpec(memory_space=pltpu.HBM)] * 2,
+        scratch_shapes=[vmem((128, 128), F32), dma((9,))],
+        cost_estimate=pl.CostEstimate(flops=0, bytes_accessed=5 * 10**6, transcendentals=0),
+        compiler_params=pltpu.CompilerParams(vmem_limit_bytes=8 * 2**20),
+        name="write_out",
+    )(*(pltpu.with_memory_space_constraint(value, vmem) for value in (mixed, received)))
     return mixed.reshape(LEV, TRC, 8, 128), bottoms.reshape(TRC, 1, ALL * 16)
 
 

time: 51.2 us -> 39.5 us (0.77)
  Pallas kernels: 46.4 us -> 38.7 us
  local copies, waits for them, and re-layouts: 4.02 us -> 0 us
    pallas_call x1 -> x2, Pallas kernels: 46.4 us -> 38.7 us  [the longest x1 37.2 us: shards(): pl.pallas_call(kernel, out_shape=[vmem((ROWS, 128), F32), vmem((128, 128)...]
    unnamed x4 -> x0, local copies, waits for them, and re-layouts: 4.02 us -> none
where the time goes in v2:
time: 39.5 us; the launch traced here: 39.3 us
  Pallas kernels  38.7 us (98%)
  between operations  0.64 us (2%)
    pallas_call x1, Pallas kernels, shards(): pl.pallas_call(kernel, out_shape=[vmem((ROWS, 128), F32), vmem((128, 128)...  37.2 us
    pallas_call x1, Pallas kernels, shards(): pl.pallas_call(finish, out_shape=[jax.ShapeDtypeStruct((ROWS, 128), F32),...  1.49 us

profile of v2, /device:TPU:1, one launch (start us, length us, event | category | flops | bytes accessed | tf_op | source)
XLA Modules:
  0.0 39.3 jit_solution(14325574839479150140)
XLA Ops:
  0.6 37.2 %tracer_step.1 = (f32[4608,128]{1,0:T(8,128)S(1)}, f32[128,128]{1,0:T(8,128)S(1)}) custom-call(f32[4608,128]{1,0:T(8,128)} %bitcast.8, f32[576,128]{1,0:T(8,128)} %bitcast.11, f32[576,128]{1,0:T(8,128)} %bitcast.12, f32[8,128]{1,0:T(8,128)} %pm_h.1, f32[1152,128]{1,0:T(8,128)} %bitcast.10, s32[8,128]{1,0:T(8,128)} %bitcast.14, s32[8,128]{1,0:T(8,128)} %bitcast.15, ...), custom_call_target="tpu_custom_call" | custom-call | flops 2000000000 | bytes 7000000 | tf_op jit(solution)/shard_map/tracer_step/pallas_call | solution.py:432
  37.9 1.5 %write_out.1 = (f32[4608,128]{1,0:T(8,128)}, f32[128,128]{1,0:T(8,128)}) custom-call(f32[4608,128]{1,0:T(8,128)S(1)} %get-tuple-element.6.mixed, f32[128,128]{1,0:T(8,128)S(1)} %get-tuple-element.7.received), custom_call_target="tpu_custom_call" | custom-call | bytes 5000000 | tf_op jit(solution)/shard_map/write_out/pallas_call | solution.py:471

commit v3 on v2

--- a/solution.py
+++ b/solution.py
@@ -61,7 +61,7 @@
 
 def kernel(
     tr_h, we_h, wn_h, pm_h, df_h, dst_h, cst_h, w_h, out, rbm,
-    tr, we, wn, pm, df, dst, cst, w, xb, rb, vb, hx, acc, hy, hd, uh, minv, av, rank, chosen_by, lhs, spread, kc,
+    tr, we, wn, pm, df, dst, cst, w, xb, rb, vb, hx, acc, hy, hd, uh, av, rank, chosen_by, lhs, spread, kc,
     inv_t, low_t, up_t, inv_b, low_b, up_b, sb,
     local_sem, ks, kr, ko, hs, hr, ys, yr, ds, dr, bs, br, bo,
 ):
@@ -77,19 +77,22 @@
             to_d = to_z * 8 + lax.rem(y + i // 2 + 1, 4) * 2 + lax.rem(core + i + 1, 2)
             act(to_g * DEV + to_d, (to_g, to_d))
 
-    def for_peers(act, beside=None):
-        for turn, step in enumerate((2, 1, 3, 0)):
+    def for_peers(act, steps=(2, 1, 3, 0), beside=None):
+        for turn, step in enumerate(steps):
 
             def some(t, carry):
-                eight(step, t, act)
+                eight(step, 2 * t, act)
+                eight(step, 2 * t + 1, act)
                 if beside is not None:
-                    beside(4 * turn + t)
+                    beside(2 * turn + t)
                 return carry
 
-            lax.fori_loop(0, 3 if step == 0 else 4, some, 0)
-        eight(0, 3, act, 7)
-        if beside is not None:
-            beside(15)
+            lax.fori_loop(0, 1 if step == 0 else 2, some, 0)
+            if step == 0:
+                eight(0, 2, act)
+                eight(0, 3, act, 7)
+                if beside is not None:
+                    beside(2 * turn + 1)
 
     loads = [
         pltpu.make_async_copy(src, dst_ref, local_sem.at[i])
@@ -105,6 +108,8 @@
     def greet(p, where):
         pl.semaphore_signal(barrier, inc=1, device_id=where, device_id_type=MESH)
 
+    for_peers(greet, (2, 1))
+
     loads[0].wait()
     xb2, rb2 = xb.reshape(ALL * 16, 128), rb.reshape(ALL * 16, 128)
 
@@ -113,16 +118,26 @@
             rows = df[pl.ds(group * 128 + tile, 8, stride=16), :]
             xb2[pl.ds(tile * 128 + group, 8, stride=16), :] = swap_blocks(rows, last=True)
 
-    for_peers(greet, pack)
+    def pack_four(part):
+        for i in range(4):
+            pack(4 * part + i)
+
+    for_peers(greet, (3, 0), pack_four)
     own = pltpu.make_async_copy(xb.at[me, pl.ds(0, 9)], rb.at[me, pl.ds(0, 9)], ko)
     own.start()
 
+    def send_kappa(p, where):
+        pltpu.make_async_remote_copy(
+            xb.at[p, pl.ds(0, 9)], rb.at[me, pl.ds(0, 9)], ks, kr, device_id=where, device_id_type=MESH
+        ).start()
+
     for copy in loads[1:]:
         copy.wait()
+    pl.semaphore_wait(barrier, ALL - 1)
     for x in range(8):
         vb[0, x] = jnp.broadcast_to(pm[x : x + 1, :], (8, 128))
 
-    def advect(block, carry):
+    def advect(block):
         first = block * 8
         cells = [
             [tr[pl.ds((first + j) * 64 + x, 8, stride=8), :] for x in range(8)] for j in range(8)
@@ -138,14 +153,15 @@
                 row = (j * 8 + x) * 8
                 moved = cells[j][x] - (we[at, :] * east + wn[at, :] * north[row : row + 8])
                 vb[1 + first + j, x] = pm[x : x + 1, :] * moved
-        return carry
-
-    lax.fori_loop(0, 9, advect, 0)
+
+    for_peers(send_kappa, beside=advect)
+    advect(8)
 
     lane = iota((8, 128), 1)
+    zero = jnp.zeros((8, 128), F32)
 
     def gather_edges(x, carry):
-        first = last = jnp.zeros((8, 128), F32)
+        first = last = zero
         for s in range(LEV + 1):
             value = pltpu.roll(vb[s, x], s + 1, 1)
             first = jnp.where(lane == s + 1, value, first)
@@ -168,16 +184,8 @@
             (acc.at[0, 0], hd.at[3], ds.at[3], dr.at[3], (down_g, down_d)),
         )
     ]
-    pl.semaphore_wait(barrier, ALL - 1)
     for copy in edge_copies:
         copy.start()
-
-    def send_kappa(p, where):
-        pltpu.make_async_remote_copy(
-            xb.at[p, pl.ds(0, 9)], rb.at[me, pl.ds(0, 9)], ks, kr, device_id=where, device_id_type=MESH
-        ).start()
-
-    for_peers(send_kappa)
     row_copies = [
         [
             pltpu.make_async_remote_copy(
@@ -208,46 +216,26 @@
         chosen_by[ALL:, at] = chosen
         before = before + counts[:, 128:]
 
-    for copy in edge_copies:
-        copy.wait()
-    sides = []
-    for side in range(2):
-        middle = hy[side, 3] + hy[side, 4]
-        rows = [hy[side, x] for x in range(8)]
-        rows[0] = rows[0] + hd[2 * side]
-        rows[7] = rows[7] + hd[2 * side + 1]
-        rows[3] = rows[4] = middle
-        sides.append(rows)
-    even = lane % 2 == 0
-    for x in range(8):
-        from_left, from_right = sides[0][x], pltpu.roll(sides[1][x], 126, 1)
-        uh[0, x] = jnp.where(even, from_left, from_right)
-        uh[1, x] = jnp.where(even, from_right, from_left)
-
     at_first, at_last = lane % 4 == 0, lane % 4 == 3
-    at_end, at_side = (lane == 0) | (lane == 127), at_first | at_last
-
-    def across(s, x, u):
-        halo = pltpu.roll(uh[lax.rem(s, 2), x], lax.rem(128 - s, 128), 1)
+    at_first, at_last = at_first & (lane > 0), at_last & (lane < 127)
+    at_side = at_first | at_last
+
+    def across(u):
         beside = jnp.where(at_first, pltpu.roll(u, 1, 1), pltpu.roll(u, 127, 1))
-        return u + jnp.where(at_side, jnp.where(at_end, halo, beside), 0.0)
-
-    def inner_sum(s):
-        middle = across(s, 3, vb[s, 3] + vb[s, 4])
-        return [(3, middle), (4, middle)] + [(x, across(s, x, vb[s, x])) for x in (1, 2, 5, 6)]
-
-    def outer_sum(s):
-        return [(x, across(s, x, vb[s, x] + hx[side, s])) for side, x in ((0, 0), (1, 7))]
-
-    for x, value in inner_sum(jnp.int32(0)):
-        minv[x] = 1.0 / value
-
-    def average_inner(s, carry):
-        for x, value in inner_sum(s):
-            av[pl.ds((s - 1) * 64 + x, 8, stride=8), :] = value * minv[x]
+        return u + jnp.where(at_side, beside, 0.0)
+
+    def put(s, x, value):
+        av[pl.ds(s * 64 + x, 8, stride=8), :] = value
+
+    def sum_inner(s, carry):
+        middle = across(vb[s, 3] + vb[s, 4])
+        put(s, 3, middle)
+        put(s, 4, middle)
+        for x in (1, 2, 5, 6):
+            put(s, x, across(vb[s, x]))
         return carry
 
-    lax.fori_loop(1, LEV + 1, average_inner, 0, unroll=4)
+    lax.fori_loop(0, LEV + 1, sum_inner, 0, unroll=4)
 
     own.wait()
     sized = rb.at[pl.ds(0, ALL - 1), pl.ds(0, 9)]
@@ -297,28 +285,48 @@
         up_b[tile(kk), :] = up2
         return up * e, next_t, up2 * e_b, next_b
 
-    zero = jnp.zeros((8, 128), F32)
-    carry = (zero,) * 4
+    lax.fori_loop(0, LEV, eliminate, (zero,) * 4, unroll=4)
+
     for part, (lo, hi) in enumerate(CUTS):
         for copy in row_copies[part]:
             copy.wait_recv()
-        if part == 0:
-            for x, value in outer_sum(jnp.int32(0)):
-                minv[x] = 1.0 / value
-
-        def both(s, carry):
-            for x, value in outer_sum(s):
-                av[pl.ds((s - 1) * 64 + x, 8, stride=8), :] = value * minv[x]
-            return eliminate(s - 1, carry)
-
-        carry = lax.fori_loop(max(lo, 1), hi, both, carry, unroll=4)
+
+        def sum_outer(s, carry):
+            for side, x in ((0, 0), (1, 7)):
+                put(s, x, across(vb[s, x] + hx[side, s]))
+            return carry
+
+        lax.fori_loop(lo, hi, sum_outer, 0, unroll=4)
+
+    for copy in edge_copies:
+        copy.wait()
+    for side in range(2):
+        middle = hy[side, 3] + hy[side, 4]
+        hy[side, 0] = hy[side, 0] + hd[2 * side]
+        hy[side, 7] = hy[side, 7] + hd[2 * side + 1]
+        hy[side, 3] = middle
+        hy[side, 4] = middle
+    even, at_end = lane % 2 == 0, (lane == 0) | (lane == 127)
+    hy2 = hy.reshape(2 * 64, 128)
+    for f in range(TRC):
+        from_left = hy2[pl.ds(f, 8, stride=8), :]
+        from_right = pltpu.roll(hy2[pl.ds(64 + f, 8, stride=8), :], 126, 1)
+        uh[0, f] = jnp.where(even, from_left, from_right)
+        uh[1, f] = jnp.where(even, from_right, from_left)
+
+    def whole(s, f):
+        halo = pltpu.roll(uh[lax.rem(s, 2), f], lax.rem(128 - s, 128), 1)
+        return av[pl.ds(pl.multiple_of(s * 64 + f * 8, 8), 8), :] + jnp.where(at_end, halo, 0.0)
+
+    share = 1.0 / whole(jnp.int32(0), 0)
 
     def at_level(k, f):
-        return pl.ds(pl.multiple_of(k * 64 + f * 8, 8), 8)
+        return pl.ds(pl.multiple_of((k + 1) * 64 + f * 8, 8), 8)
 
     def sweep_1(k, previous):
         inv, low = inv_t[tile(k), :], low_t[tile(k), :]
-        current = tuple(av[at_level(k, f), :] * inv + low * previous[f] for f in range(TRC))
+        inv = inv * share
+        current = tuple(whole(k + 1, f) * inv + low * previous[f] for f in range(TRC))
         for f in range(TRC):
             av[at_level(k, f), :] = current[f]
         return current
@@ -355,7 +363,7 @@
 
     slots = iota((16, 128), 0)
     for f in range(TRC):
-        base = av[(LEV - 1) * 64 + f * 8 : (LEV - 1) * 64 + f * 8 + 8, :]
+        base = av[LEV * 64 + f * 8 : LEV * 64 + f * 8 + 8, :]
         rest = base - base.astype(BF16).astype(F32)
         for x in range(8):
             hit = jnp.broadcast_to(rank[x : x + 1, :], (16, 128)) == slots
@@ -382,7 +390,7 @@
         up = jnp.where(third, up_t[tile(k), :], 0.0)
         solved = tuple(av[at_level(k, f), :] + up * following[f] for f in range(TRC))
         for f in range(TRC):
-            out[at_level(k, f), :] = solved[f]
+            out[pl.ds(pl.multiple_of(k * 64 + f * 8, 8), 8), :] = solved[f]
         return solved
 
     lax.fori_loop(0, LEV, sweep_4, (zero,) * TRC, unroll=4)
@@ -451,8 +459,7 @@
             vmem((2, 8, 8, 128), F32),
             vmem((4, 8, 128), F32),
             vmem((2, 8, 8, 128), F32),
-            vmem((8, 8, 128), F32),
-            vmem((ROWS, 128), F32),
+            vmem((ROWS + 64, 128), F32),
             vmem((8, 128), jnp.int32),
             vmem((2 * ALL, 1024), BF16),
             vmem((LEV * 16, 2 * ALL), BF16),

time: 39.5 us -> 37.8 us (0.957)
  Pallas kernels: 38.7 us -> 37.1 us
    pallas_call x1, Pallas kernels: 37.2 us -> 35.6 us  [shards(): pl.pallas_call(kernel, out_shape=[vmem((ROWS, 128), F32), vmem((128, 128)...]
where the time goes in v3:
time: 37.8 us; the launch traced here: 37.7 us
  Pallas kernels  37.1 us (98%)
  between operations  0.64 us (2%)
    pallas_call x1, Pallas kernels, shards(): pl.pallas_call(kernel, out_shape=[vmem((ROWS, 128), F32), vmem((128, 128)...  35.6 us
    pallas_call x1, Pallas kernels, shards(): pl.pallas_call(finish, out_shape=[jax.ShapeDtypeStruct((ROWS, 128), F32),...  1.49 us

profile of v3, /device:TPU:1, one launch (start us, length us, event | category | flops | bytes accessed | tf_op | source)
XLA Modules:
  0.0 37.7 jit_solution(16519798056113785316)
XLA Ops:
  0.6 35.6 %tracer_step.1 = (f32[4608,128]{1,0:T(8,128)S(1)}, f32[128,128]{1,0:T(8,128)S(1)}) custom-call(f32[4608,128]{1,0:T(8,128)} %bitcast.8, f32[576,128]{1,0:T(8,128)} %bitcast.11, f32[576,128]{1,0:T(8,128)} %bitcast.12, f32[8,128]{1,0:T(8,128)} %pm_h.1, f32[1152,128]{1,0:T(8,128)} %bitcast.10, s32[8,128]{1,0:T(8,128)} %bitcast.14, s32[8,128]{1,0:T(8,128)} %bitcast.15, ...), custom_call_target="tpu_custom_call" | custom-call | flops 2000000000 | bytes 7000000 | tf_op jit(solution)/shard_map/tracer_step/pallas_call | solution.py:440
  36.2 1.5 %write_out.1 = (f32[4608,128]{1,0:T(8,128)}, f32[128,128]{1,0:T(8,128)}) custom-call(f32[4608,128]{1,0:T(8,128)S(1)} %get-tuple-element.6.mixed, f32[128,128]{1,0:T(8,128)S(1)} %get-tuple-element.7.received), custom_call_target="tpu_custom_call" | custom-call | bytes 5000000 | tf_op jit(solution)/shard_map/write_out/pallas_call | solution.py:478

commit v4 on v3

--- a/solution.py
+++ b/solution.py
@@ -231,7 +231,7 @@
         middle = across(vb[s, 3] + vb[s, 4])
         put(s, 3, middle)
         put(s, 4, middle)
-        for x in (1, 2, 5, 6):
+        for x in (0, 1, 2, 5, 6, 7):
             put(s, x, across(vb[s, x]))
         return carry
 
@@ -261,6 +261,33 @@
         return carry
 
     lax.fori_loop(0, 4, columns, 0)
+
+    for copy in edge_copies:
+        copy.wait()
+    for side in range(2):
+        middle = hy[side, 3] + hy[side, 4]
+        hy[side, 0] = hy[side, 0] + hd[2 * side]
+        hy[side, 7] = hy[side, 7] + hd[2 * side + 1]
+        hy[side, 3] = middle
+        hy[side, 4] = middle
+    even, at_end = lane % 2 == 0, (lane == 0) | (lane == 127)
+    hy2 = hy.reshape(2 * 64, 128)
+    for f in range(TRC):
+        from_left = hy2[pl.ds(f, 8, stride=8), :]
+        from_right = pltpu.roll(hy2[pl.ds(64 + f, 8, stride=8), :], 126, 1)
+        uh[0, f] = jnp.where(even, from_left, from_right)
+        uh[1, f] = jnp.where(even, from_right, from_left)
+
+    def add_lanes(s):
+        shift, parity = lax.rem(128 - s, 128), lax.rem(s, 2)
+        for f in range(TRC):
+            at = pl.ds(pl.multiple_of(s * 64 + f * 8, 8), 8)
+            av[at, :] = av[at, :] + jnp.where(at_end, pltpu.roll(uh[parity, f], shift, 1), 0.0)
+
+    def sum_outer(s):
+        for side, x in ((0, 0), (1, 7)):
+            at = pl.ds(s * 64 + x, 8, stride=8)
+            av[at, :] = av[at, :] + across(hx[side, s])
 
     def tile(k):
         return pl.ds(pl.multiple_of(k * 8, 8), 8)
@@ -285,53 +312,33 @@
         up_b[tile(kk), :] = up2
         return up * e, next_t, up2 * e_b, next_b
 
-    lax.fori_loop(0, LEV, eliminate, (zero,) * 4, unroll=4)
-
-    for part, (lo, hi) in enumerate(CUTS):
-        for copy in row_copies[part]:
-            copy.wait_recv()
-
-        def sum_outer(s, carry):
-            for side, x in ((0, 0), (1, 7)):
-                put(s, x, across(vb[s, x] + hx[side, s]))
-            return carry
-
-        lax.fori_loop(lo, hi, sum_outer, 0, unroll=4)
-
-    for copy in edge_copies:
-        copy.wait()
-    for side in range(2):
-        middle = hy[side, 3] + hy[side, 4]
-        hy[side, 0] = hy[side, 0] + hd[2 * side]
-        hy[side, 7] = hy[side, 7] + hd[2 * side + 1]
-        hy[side, 3] = middle
-        hy[side, 4] = middle
-    even, at_end = lane % 2 == 0, (lane == 0) | (lane == 127)
-    hy2 = hy.reshape(2 * 64, 128)
-    for f in range(TRC):
-        from_left = hy2[pl.ds(f, 8, stride=8), :]
-        from_right = pltpu.roll(hy2[pl.ds(64 + f, 8, stride=8), :], 126, 1)
-        uh[0, f] = jnp.where(even, from_left, from_right)
-        uh[1, f] = jnp.where(even, from_right, from_left)
-
-    def whole(s, f):
-        halo = pltpu.roll(uh[lax.rem(s, 2), f], lax.rem(128 - s, 128), 1)
-        return av[pl.ds(pl.multiple_of(s * 64 + f * 8, 8), 8), :] + jnp.where(at_end, halo, 0.0)
-
-    share = 1.0 / whole(jnp.int32(0), 0)
 
     def at_level(k, f):
         return pl.ds(pl.multiple_of((k + 1) * 64 + f * 8, 8), 8)
 
+    for pair in row_copies:
+        for copy in pair:
+            copy.wait_recv()
+    sum_outer(jnp.int32(0))
+    add_lanes(jnp.int32(0))
+
+    def complete(s, carry):
+        sum_outer(s)
+        add_lanes(s)
+        return eliminate(s - 1, carry)
+
+    lax.fori_loop(1, LEV + 1, complete, (zero,) * 4, unroll=4)
+    share = 1.0 / av[:8, :]
+
     def sweep_1(k, previous):
-        inv, low = inv_t[tile(k), :], low_t[tile(k), :]
-        inv = inv * share
-        current = tuple(whole(k + 1, f) * inv + low * previous[f] for f in range(TRC))
+        inv, low = inv_t[tile(k), :] * share, low_t[tile(k), :]
+        current = tuple(av[at_level(k, f), :] * inv + low * previous[f] for f in range(TRC))
         for f in range(TRC):
             av[at_level(k, f), :] = current[f]
         return current
 
     lax.fori_loop(0, LEV, sweep_1, (zero,) * TRC, unroll=4)
+
     second, third = cst[...] >= 2, cst[...] >= 3
 
     def sweep_2(i, carry):

time: 37.8 us -> 38 us (level)
  no operation moved by 1% of the time
where the time goes in v4:
time: 38 us; the launch traced here: 37.9 us
  Pallas kernels  37.2 us (98%)
  between operations  0.64 us (2%)
    pallas_call x1, Pallas kernels, shards(): pl.pallas_call(kernel, out_shape=[vmem((ROWS, 128), F32), vmem((128, 128)...  35.7 us
    pallas_call x1, Pallas kernels, shards(): pl.pallas_call(finish, out_shape=[jax.ShapeDtypeStruct((ROWS, 128), F32),...  1.49 us

profile of v4, /device:TPU:1, one launch (start us, length us, event | category | flops | bytes accessed | tf_op | source)
XLA Modules:
  0.0 37.9 jit_solution(5847018544626001159)
XLA Ops:
  0.6 35.7 %tracer_step.1 = (f32[4608,128]{1,0:T(8,128)S(1)}, f32[128,128]{1,0:T(8,128)S(1)}) custom-call(f32[4608,128]{1,0:T(8,128)} %bitcast.8, f32[576,128]{1,0:T(8,128)} %bitcast.11, f32[576,128]{1,0:T(8,128)} %bitcast.12, f32[8,128]{1,0:T(8,128)} %pm_h.1, f32[1152,128]{1,0:T(8,128)} %bitcast.10, s32[8,128]{1,0:T(8,128)} %bitcast.14, s32[8,128]{1,0:T(8,128)} %bitcast.15, ...), custom_call_target="tpu_custom_call" | custom-call | flops 2000000000 | bytes 7000000 | tf_op jit(solution)/shard_map/tracer_step/pallas_call | solution.py:447
  36.4 1.5 %write_out.1 = (f32[4608,128]{1,0:T(8,128)}, f32[128,128]{1,0:T(8,128)}) custom-call(f32[4608,128]{1,0:T(8,128)S(1)} %get-tuple-element.6.mixed, f32[128,128]{1,0:T(8,128)S(1)} %get-tuple-element.7.received), custom_call_target="tpu_custom_call" | custom-call | bytes 5000000 | tf_op jit(solution)/shard_map/write_out/pallas_call | solution.py:485
